TPU v7x, 512 devices: a whole 4x4x16 slice. The times are simulated.
512 devices in a mesh: seq: 128 (over z, y, core), grp: 4 (over x).
Axes of the slice: x: 4, y: 4, z: 16, core: 2. Of those that a mesh axis runs over, the one named last changes fastest.
Arguments:
- tokens: bfloat16 [131072, 512], P('seq'), may hold values from -12 to 12
- w_qkv: bfloat16 [3, 512, 512], P(None, None, 'grp'), may hold values from -0.25 to 0.25
- w_out: bfloat16 [512, 512], replicated, may hold values from -0.75 to 0.75
- w_up: bfloat16 [512, 2048], P(None, 'grp'), may hold values from -0.25 to 0.25
- w_down: bfloat16 [2048, 512], P('grp'), may hold values from -0.125 to 0.125
- score_scale: float32 [8], P('grp'), may hold values from 8 to 400
- patch_list: int32 [128, 3], P('seq'), may hold values from 0 to 127, as said below
- relay_dest: int32 [131072, 1], P('seq'), may hold values from 0 to 127; in each aligned block of 1024 rows (0 to 1023, 1024 to 2047, ...) at most 16 rows name the same one
Outputs:
- relayed: bfloat16 [262144, 512], P('seq', 'grp')
Inputs may be any that keep to these rules, and one draw needn't show every extreme that they name: `patch_list`: row p lists patch p first, then 3 - 1 other distinct patches, each at most 2 patches away from p. `relay_dest`: the rows of one block of 1024 tokens name any one block at most 16 times; in every draw some block names some block exactly 16 times.
All inputs are finite; a program needn't handle non-finite values.
Results may differ from a plain program's by a relative error of at most 0.017.
Values may be sent and summed in bfloat16 or wider, within the bound.
A program may use at most 64 MiB of HBM per device.

v0:
```python
import jax
import jax.numpy as jnp
from jax import lax
from jax.sharding import PartitionSpec as P

PATCH = 1024
REACH = 2
NB = 3


def shifted(block, axis, distance):
    devices = range(lax.axis_size(axis))
    route = [(i - distance, i) for i in devices if i - distance in devices]
    return lax.ppermute(block, axis, route)


def layer_norm(token_rows):
    row_mean = jnp.mean(token_rows, axis=-1, keepdims=True)
    spread = jnp.mean(token_rows * token_rows, axis=-1, keepdims=True) - row_mean * row_mean
    return (token_rows - row_mean) * lax.rsqrt(spread + 1e-05)


def unit_heads(values, head_dim):
    shaped = values.reshape(values.shape[0], -1, head_dim)
    scaled = shaped * lax.rsqrt(jnp.mean(shaped * shaped, axis=-1, keepdims=True) + 1e-06)
    return scaled.reshape(values.shape)


def project(token_rows, weights):
    normed = layer_norm(token_rows.astype(jnp.float32)).astype(jnp.bfloat16)
    return jnp.einsum("nd,cde->cne", normed, weights, preferred_element_type=jnp.float32)


def body(tokens, w_qkv, w_out, w_up, w_down, score_scale, patch_list, relay_dest):
    n_seq = lax.axis_size("seq")
    seq_index = lax.axis_index("seq")
    grp_index = lax.axis_index("grp")
    tok_dev, model_width = tokens.shape
    quarter = w_qkv.shape[2]
    heads_dev = score_scale.shape[0]
    head_dim = quarter // heads_dev
    patch_dev = tok_dev // PATCH
    hop_count = -(-REACH // patch_dev)
    offsets = [offset for offset in range(-hop_count, hop_count + 1) if offset != 0]
    own_products = project(tokens, w_qkv)
    queries = unit_heads(own_products[0], head_dim).astype(jnp.bfloat16)
    key_rows = unit_heads(own_products[1], head_dim).astype(jnp.bfloat16)
    value_rows = own_products[2].astype(jnp.bfloat16)
    fetched_pairs = [shifted((key_rows, value_rows), "seq", -offset) for offset in offsets]
    near_keys = [fetched_pair[0] for fetched_pair in fetched_pairs]
    near_values = [fetched_pair[1] for fetched_pair in fetched_pairs]
    window_keys = jnp.concatenate(near_keys[:hop_count] + [key_rows] + near_keys[hop_count:], 0)
    window_values = jnp.concatenate(
        near_values[:hop_count] + [value_rows] + near_values[hop_count:], 0
    )
    window_count = 2 * hop_count + 1
    key_patches = window_keys.reshape(window_count * patch_dev, PATCH, quarter)
    value_patches = window_values.reshape(window_count * patch_dev, PATCH, quarter)
    first_patch = (seq_index - hop_count) * patch_dev
    relative = patch_list - first_patch
    listed_keys = key_patches[relative].reshape(patch_dev, NB * PATCH, quarter)
    listed_values = value_patches[relative].reshape(patch_dev, NB * PATCH, quarter)
    block_rows = min(512, PATCH)
    block_count = PATCH // block_rows
    query_blocks = queries.reshape(patch_dev, block_count, block_rows, quarter)
    factors = score_scale / head_dim

    def attend(item_index):
        patch_index = item_index // (heads_dev * block_count)
        head_index = item_index // block_count % heads_dev
        block_index = item_index % block_count
        query_block = lax.dynamic_slice_in_dim(
            query_blocks[patch_index, block_index], head_index * head_dim, head_dim, 1
        )
        key_block = lax.dynamic_slice_in_dim(
            listed_keys[patch_index], head_index * head_dim, head_dim, 1
        )
        value_block = lax.dynamic_slice_in_dim(
            listed_values[patch_index], head_index * head_dim, head_dim, 1
        )
        scores = lax.dot_general(
            query_block, key_block, (((1,), (1,)), ((), ())), preferred_element_type=jnp.float32
        )
        scores = scores * factors[head_index]
        row_top = jnp.max(scores, axis=1, keepdims=True)
        exponent = jnp.exp(scores - row_top)
        row_total = jnp.sum(exponent, axis=1, keepdims=True)
        weighted = jnp.dot(
            exponent.astype(jnp.bfloat16), value_block, preferred_element_type=jnp.float32
        )
        return (weighted / row_total).astype(jnp.bfloat16)

    attended = lax.map(attend, jnp.arange(patch_dev * heads_dev * block_count, dtype=jnp.int32))
    attended = attended.reshape(patch_dev, heads_dev, block_count, block_rows, head_dim)
    attended = attended.transpose(0, 2, 3, 1, 4).reshape(tok_dev, quarter)
    head_weights = lax.dynamic_slice_in_dim(w_out, grp_index * quarter, quarter, 0)
    partial_proj = jnp.dot(attended, head_weights, preferred_element_type=jnp.float32)
    proj_share = lax.psum_scatter(
        partial_proj.astype(jnp.bfloat16), "grp", scatter_dimension=1, tiled=True
    ).astype(jnp.float32)
    token_share = lax.dynamic_slice_in_dim(tokens, grp_index * quarter, quarter, 1).astype(
        jnp.float32
    )
    resid = (token_share + proj_share).astype(jnp.bfloat16)
    resid_wide = resid.astype(jnp.float32)
    row_sums = lax.psum(
        (jnp.sum(resid_wide, axis=1), jnp.sum(resid_wide * resid_wide, axis=1)), "grp"
    )
    row_mean = row_sums[0] / model_width
    spread = row_sums[1] / model_width - row_mean * row_mean
    normed_share = ((resid_wide - row_mean[:, None]) * lax.rsqrt(spread + 1e-05)[:, None]).astype(
        jnp.bfloat16
    )
    hidden_pre = jnp.dot(
        lax.all_gather(normed_share, "grp", axis=1, tiled=True),
        w_up,
        preferred_element_type=jnp.float32,
    )
    hidden = jax.nn.gelu(hidden_pre).astype(jnp.bfloat16)
    partial_down = jnp.dot(hidden, w_down, preferred_element_type=jnp.float32)
    down_share = lax.psum_scatter(
        partial_down.astype(jnp.bfloat16), "grp", scatter_dimension=1, tiled=True
    ).astype(jnp.float32)
    out_rows = (resid.astype(jnp.float32) + down_share).astype(jnp.bfloat16)
    capacity = 2 * tok_dev // n_seq
    destination = relay_dest[:, 0]
    onehot = (destination[:, None] == jnp.arange(n_seq, dtype=jnp.int32)[None, :]).astype(jnp.int32)
    before = jnp.cumsum(onehot, axis=0) - onehot
    rank_rows = jnp.sum(before * onehot, axis=1)
    slot_index = destination * capacity + rank_rows
    send_buffer = jnp.zeros((n_seq * capacity, quarter), jnp.bfloat16).at[slot_index].set(out_rows)
    received = lax.all_to_all(
        send_buffer.reshape(n_seq, capacity, quarter),
        "seq",
        split_axis=0,
        concat_axis=0,
        tiled=True,
    )
    return received.reshape(n_seq * capacity, quarter)


def solution(mesh):
    return jax.shard_map(
        body,
        mesh=mesh,
        in_specs=(
            P("seq", None),
            P(None, None, "grp"),
            P(),
            P(None, "grp"),
            P("grp", None),
            P("grp"),
            P("seq", None),
            P("seq", None),
        ),
        out_specs=P("seq", "grp"),
        check_vma=False,
    )
```

profile of v0, /device:TPU:33, one launch (start us, length us, event | category | flops | bytes accessed | tf_op | source)
XLA Modules:
  0.0 282.7 jit_solution(186942135605513350)
XLA Ops:
  9.4 2.0 fusion.36
  13.7 3.2 %collective-permute-start = (bf16[1024,128]{0,1:T(8,128)(2,1)S(1)}, bf16[1024,128]{0,1:T(8,128)(2,1)}, u32[]{:S(2)}, u32[]{:S(2)}) collective-permute-start(bf16[1024,128]{0,1:T(8,128)(2,1)S(1)} %fusion.50), channel_id=1, source_target_pairs={{0,8},{4,12},{8,16},{12,20},{16,24},{20,28},{24,32},{28,36},{32,40... | collective-permute-start | bytes 786440 | tf_op jit(solution)/shard_map/ppermute | solution.py:14
  16.9 4.0 %collective-permute-start.1 = (bf16[1024,128]{0,1:T(8,128)(2,1)S(1)}, bf16[1024,128]{0,1:T(8,128)(2,1)}, u32[]{:S(2)}, u32[]{:S(2)}) collective-permute-start(bf16[1024,128]{0,1:T(8,128)(2,1)S(1)} %fusion.50), channel_id=1, source_target_pairs={{0,4},{4,8},{8,12},{12,16},{16,20},{20,24},{24,28},{28,32},{32,36}... | collective-permute-start | bytes 786440 | tf_op jit(solution)/shard_map/ppermute | solution.py:14
  21.0 1.9 collective-permute-start.2
  22.9 4.2 %collective-permute-start.3 = (bf16[1024,128]{0,1:T(8,128)(2,1)S(1)}, bf16[1024,128]{0,1:T(8,128)(2,1)}, u32[]{:S(2)}, u32[]{:S(2)}) collective-permute-start(bf16[1024,128]{0,1:T(8,128)(2,1)S(1)} %fusion.50), channel_id=1, source_target_pairs={{8,0},{12,4},{16,8},{20,12},{24,16},{28,20},{32,24},{36,28},{40,32... | collective-permute-start | bytes 786440 | tf_op jit(solution)/shard_map/ppermute | solution.py:14
  27.9 1.9 collective-permute-start.4
  31.2 3.9 %collective-permute-start.5 = (bf16[1024,128]{0,1:T(8,128)(2,1)}, bf16[1024,128]{0,1:T(8,128)(2,1)S(1)}, u32[]{:S(2)}, u32[]{:S(2)}) collective-permute-start(bf16[1024,128]{0,1:T(8,128)(2,1)} %fusion.53), channel_id=1, source_target_pairs={{0,4},{4,8},{8,12},{12,16},{16,20},{20,24},{24,28},{28,32},{32,36}... | collective-permute-start | bytes 786440 | tf_op jit(solution)/shard_map/ppermute | solution.py:14
  36.1 2.3 collective-permute-start.6
  39.4 5.4 %collective-permute-start.7 = (bf16[1024,128]{0,1:T(8,128)(2,1)}, bf16[1024,128]{0,1:T(8,128)(2,1)S(1)}, u32[]{:S(2)}, u32[]{:S(2)}) collective-permute-start(bf16[1024,128]{0,1:T(8,128)(2,1)} %fusion.53), channel_id=1, source_target_pairs={{8,0},{12,4},{16,8},{20,12},{24,16},{28,20},{32,24},{36,28},{40,32... | collective-permute-start | bytes 786440 | tf_op jit(solution)/shard_map/ppermute | solution.py:14
  55.4 2.4 copy.26
  58.5 2.0 gather_fusion.1
  60.5 39.8 %while.13 = (s32[]{:T(128)}, bf16[4,512,64]{1,2,0:T(8,128)(2,1)S(1)}, s32[4]{0:T(128)S(1)}, bf16[1,2,512,128]{2,1,3,0:T(2,128)(2,1)S(1)}, bf16[1,3072,128]{2,1,0...) while((s32[]{:T(128)}, ...), condition=%wide.region_10.11_spmd, body=%wide.region_7.10_spmd.sunk | while | flops 415300672 | bytes 20851312 | solution.py:93
  64.7 1.8 multiply_reduce_fusion.2
  68.3 2.2 fusion.79
  78.2 2.2 fusion.79
  88.2 2.2 fusion.79
  98.2 2.2 fusion.79
  102.6 34.9 %reduce-scatter.7.cloned.1.call-done = bf16[128,1024]{1,0:T(8,128)(2,1)} async-done(((bf16[512,1024]{1,0:T(8,128)(2,1)}), bf16[128,1024]{1,0:T(8,128)(2,1)}) %reduce-scatter.7.cloned.1.call-update) | async-done | bytes 262160
  140.0 6.6 %all-reduce = (f32[1024]{0:T(1024)S(1)}, f32[1024]{0:T(1024)S(1)}) all-reduce(f32[1024]{0:T(1024)S(1)} %get-tuple-element.144, f32[1024]{0:T(1024)S(1)} %get-tuple-element.143), channel_id=1, replica_groups=mesh['seq'=128,'grp'=4] {'grp'}, use_global_device_ids=true, to_apply=%region_15.16 | all-reduce | flops 2048 | bytes 16384 | tf_op jit(solution)/shard_map/psum | solution.py:106
  147.9 35.5 %all-gather.2.cloned.1.call-done = bf16[1024,512]{1,0:T(8,128)(2,1)} async-done(((bf16[1024,128]{1,0:T(8,128)(2,1)}), bf16[1024,512]{1,0:T(8,128)(2,1)}) %all-gather.2.cloned.1.call-update) | async-done | bytes 1048592 | tf_op jit(solution)/shard_map/all_gather | solution.py:115
  183.4 2.7 convolution_convert_fusion.1
  188.4 31.1 %reduce-scatter.9.cloned.1.call-done = bf16[128,1024]{1,0:T(8,128)(2,1)} async-done(((bf16[512,1024]{1,0:T(8,128)(2,1)}), bf16[128,1024]{1,0:T(8,128)(2,1)}) %reduce-scatter.9.cloned.1.call-update) | async-done | bytes 262160
  220.6 3.4 %scatter_custom_fusion = bf16[2048,128]{1,0:T(8,128)(2,1)S(1)} fusion(s32[1024]{0:T(1024)S(1)} %bitcast.114, bf16[1024,128]{1,0:T(8,128)(2,1)S(1)} %get-tuple-element.161, bf16[1024,128]{1,0:T(8,128)(2,1)S(1)} %copy.32, bf16[]{:T(256)} %constant.173.clone.1), kind=kCustom, calls=%fused_computation.67 | custom fusion | flops 524288 | bytes 1048578 | tf_op jit(solution)/shard_map/scatter | solution.py:131
  224.0 51.4 %all_to_all.5 = bf16[128,16,128]{2,1,0:T(8,128)(2,1)S(1)} all-to-all(bf16[128,16,128]{2,1,0:T(8,128)(2,1)S(1)} %bitcast.103), channel_id=1, replica_groups=mesh['seq'=128,'grp'=4] {'seq'}, dimensions={0} | all-to-all | bytes 1048576 | tf_op jit(solution)/shard_map/all_to_all | solution.py:132
  (104 shorter events, 48.8 us)
Async XLA Ops:
  6.5 94.2 %copy-start = (bf16[512,512]{1,0:T(8,128)(2,1)S(1)}, bf16[512,512]{1,0:T(8,128)(2,1)}, u32[]{:S(2)}) copy-start(bf16[512,512]{1,0:T(8,128)(2,1)} %param.12) | copy-start | bytes 1572868
  6.5 131.0 %reduce-scatter.7.cloned.1.call-start = ((), (), s32[]{:S(2)}) async-start(), calls=%async_computation.4 | async-start | bytes 1310720
  11.4 16.5 %copy-start.1 = (f32[1024,384]{0,1}, f32[1024,384]{0,1:S(1)}, u32[]{:S(2)}) copy-start(f32[1024,384]{0,1:S(1)} %fusion.36) | copy-start | bytes 4718596
  13.7 17.2 %copy-start.6 = (f32[2]{0:T(128)S(1)}, f32[2]{0:T(128)}, u32[]{:S(2)}) copy-start(f32[2]{0:T(128)} %param.15) | copy-start | bytes 28
  13.7 17.5 %collective-permute-start = (bf16[1024,128]{0,1:T(8,128)(2,1)S(1)}, bf16[1024,128]{0,1:T(8,128)(2,1)}, u32[]{:S(2)}, u32[]{:S(2)}) collective-permute-start(bf16[1024,128]{0,1:T(8,128)(2,1)S(1)} %fusion.50), channel_id=1, source_target_pairs={{0,8},{4,12},{8,16},{12,20},{16,24},{20,28},{24,32},{28,36},{32,40... | collective-permute-start | bytes 786440 | tf_op jit(solution)/shard_map/ppermute | solution.py:14
  16.9 19.2 %collective-permute-start.1 = (bf16[1024,128]{0,1:T(8,128)(2,1)S(1)}, bf16[1024,128]{0,1:T(8,128)(2,1)}, u32[]{:S(2)}, u32[]{:S(2)}) collective-permute-start(bf16[1024,128]{0,1:T(8,128)(2,1)S(1)} %fusion.50), channel_id=1, source_target_pairs={{0,4},{4,8},{8,12},{12,16},{16,20},{20,24},{24,28},{28,32},{32,36}... | collective-permute-start | bytes 786440 | tf_op jit(solution)/shard_map/ppermute | solution.py:14
  21.0 25.5 %collective-permute-start.2 = (bf16[1024,128]{0,1:T(8,128)(2,1)S(1)}, bf16[1024,128]{0,1:T(8,128)(2,1)}, u32[]{:S(2)}, u32[]{:S(2)}) collective-permute-start(bf16[1024,128]{0,1:T(8,128)(2,1)S(1)} %fusion.50), channel_id=1, source_target_pairs={{4,0},{8,4},{12,8},{16,12},{20,16},{24,20},{28,24},{32,28},{36,32}... | collective-permute-start | bytes 786440 | tf_op jit(solution)/shard_map/ppermute | solution.py:14
  22.9 24.5 %collective-permute-start.3 = (bf16[1024,128]{0,1:T(8,128)(2,1)S(1)}, bf16[1024,128]{0,1:T(8,128)(2,1)}, u32[]{:S(2)}, u32[]{:S(2)}) collective-permute-start(bf16[1024,128]{0,1:T(8,128)(2,1)S(1)} %fusion.50), channel_id=1, source_target_pairs={{8,0},{12,4},{16,8},{20,12},{24,16},{28,20},{32,24},{36,28},{40,32... | collective-permute-start | bytes 786440 | tf_op jit(solution)/shard_map/ppermute | solution.py:14
  27.9 11.5 %collective-permute-start.4 = (bf16[1024,128]{0,1:T(8,128)(2,1)}, bf16[1024,128]{0,1:T(8,128)(2,1)}, u32[]{:S(2)}, u32[]{:S(2)}) collective-permute-start(bf16[1024,128]{0,1:T(8,128)(2,1)} %fusion.53), channel_id=1, source_target_pairs={{0,8},{4,12},{8,16},{12,20},{16,24},{20,28},{24,32},{28,36},{32,40... | collective-permute-start | bytes 786440 | tf_op jit(solution)/shard_map/ppermute | solution.py:14
  29.8 1.3 copy-start.7
  31.2 17.3 %collective-permute-start.5 = (bf16[1024,128]{0,1:T(8,128)(2,1)}, bf16[1024,128]{0,1:T(8,128)(2,1)S(1)}, u32[]{:S(2)}, u32[]{:S(2)}) collective-permute-start(bf16[1024,128]{0,1:T(8,128)(2,1)} %fusion.53), channel_id=1, source_target_pairs={{0,4},{4,8},{8,12},{12,16},{16,20},{20,24},{24,28},{28,32},{32,36}... | collective-permute-start | bytes 786440 | tf_op jit(solution)/shard_map/ppermute | solution.py:14
  36.1 17.7 %collective-permute-start.6 = (bf16[1024,128]{0,1:T(8,128)(2,1)}, bf16[1024,128]{0,1:T(8,128)(2,1)S(1)}, u32[]{:S(2)}, u32[]{:S(2)}) collective-permute-start(bf16[1024,128]{0,1:T(8,128)(2,1)} %fusion.53), channel_id=1, source_target_pairs={{4,0},{8,4},{12,8},{16,12},{20,16},{24,20},{28,24},{32,28},{36,32}... | collective-permute-start | bytes 786440 | tf_op jit(solution)/shard_map/ppermute | solution.py:14
  39.4 15.2 %collective-permute-start.7 = (bf16[1024,128]{0,1:T(8,128)(2,1)}, bf16[1024,128]{0,1:T(8,128)(2,1)S(1)}, u32[]{:S(2)}, u32[]{:S(2)}) collective-permute-start(bf16[1024,128]{0,1:T(8,128)(2,1)} %fusion.53), channel_id=1, source_target_pairs={{8,0},{12,4},{16,8},{20,12},{24,16},{28,20},{32,24},{36,28},{40,32... | collective-permute-start | bytes 786440 | tf_op jit(solution)/shard_map/ppermute | solution.py:14
  48.4 1.1 copy-start.2
  102.5 80.9 %copy-start.4 = (bf16[512,512]{1,0:T(8,128)(2,1)S(1)}, bf16[512,512]{1,0:T(8,128)(2,1)}, u32[]{:S(2)}) copy-start(bf16[512,512]{1,0:T(8,128)(2,1)} %param.14) | copy-start | bytes 1572868
  102.5 80.9 %copy-start.5 = (bf16[512,512]{1,0:T(8,128)(2,1)S(1)}, bf16[512,512]{1,0:T(8,128)(2,1)}, u32[]{:S(2)}) copy-start(bf16[512,512]{1,0:T(8,128)(2,1)} %param.13) | copy-start | bytes 1572868
  102.5 80.9 %all-gather.2.cloned.1.call-start = ((), (), s32[]{:S(2)}) async-start(), calls=%async_computation.3 | async-start | bytes 1310720 | tf_op jit(solution)/shard_map/all_gather | solution.py:115
  147.7 71.8 %reduce-scatter.9.cloned.1.call-start = ((), (), s32[]{:S(2)}) async-start(), calls=%async_computation.5 | async-start | bytes 1310720
  186.1 1.4 copy-start.3
Sparse Core Ops, SparseCore 0:
  102.7 34.8 reduce-scatter.6
  147.8 35.6 all-gather.1
  187.6 31.8 reduce-scatter.8
where the time goes:
time: 284 us; the launch traced here: 283 us
  waiting for transfers between devices  102 us (36%)
  blocking collectives  58 us (20%)
  local copies, waits for them, and re-layouts  32.6 us (11%)
  starting transfers between devices  27.1 us (10%)
  matrix products  21.2 us (7%)
  other arithmetic  17.8 us (6%)
  between operations  13.6 us (5%)
  loops' own time  10.7 us (4%)
    unnamed x5, waiting for transfers between devices  66.1 us
    all_to_all x1, blocking collectives, body(): lax.all_to_all(send_buffer.reshape(n_seq, capacity, quarter), 'seq', spli...  51.4 us
    all_gather x1, waiting for transfers between devices, body(): lax.all_gather(normed_share, 'grp', axis=1, tiled=True)  35.5 us
    ppermute x8, starting transfers between devices, shifted(): return lax.ppermute(block, axis, route)  26.9 us
    unnamed x31, local copies, waits for them, and re-layouts  15.9 us
    another operation x1, loops' own time, body(): lax.map(attend, jnp.arange(patch_dev * heads_dev * block_count, dtype=jnp...  10.7 us
    dot_general x4, matrix products, attend(): jnp.dot(exponent.astype(jnp.bfloat16), value_block, preferred_element_typ...  8.91 us
    dot_general x4, matrix products, attend(): lax.dot_general(query_block, key_block, (((1,), (1,)), ((), ())), preferr...  7.2 us
  transfers between devices with their start and end apart: 11, of which 3 were waited for; matrix products, arithmetic and copies ran while one was open for 5% of the time, Pallas kernels for 0%

commit v1 on v0

--- a/solution.py
+++ b/solution.py
@@ -112,7 +112,9 @@
         jnp.bfloat16
     )
     hidden_pre = jnp.dot(
-        lax.all_gather(normed_share, "grp", axis=1, tiled=True),
+        jnp.concatenate(
+            lax.all_to_all(jnp.stack([normed_share] * lax.axis_size("grp")), "grp", 0, 0), axis=1
+        ),
         w_up,
         preferred_element_type=jnp.float32,
     )

time: 284 us -> 263 us (0.926)
  waiting for transfers between devices: 102 us -> 68.2 us
  blocking collectives: 58 us -> 71.3 us
    all_gather x1 -> x0, waiting for transfers between devices: 35.5 us -> none  [body(): lax.all_gather(normed_share, 'grp', axis=1, tiled=True)]
    all_to_all x0 -> x1, blocking collectives: none -> 13.2 us  [body(): lax.all_to_all(jnp.stack([normed_share] * lax.axis_size('grp')), 'grp', 0...]
    unnamed x5 -> x4, waiting for transfers between devices: 66.1 us -> 68.2 us
    unnamed x31 -> x29, local copies, waits for them, and re-layouts: 15.9 us -> 15.9 us
  transfers between devices with their start and end apart: 11 -> 10, of which waited for: 3 -> 2; matrix products, arithmetic and copies ran while one was open for 5% -> 5% of each run, Pallas kernels for 0% -> 0%
where the time goes in v1:
time: 263 us; the launch traced here: 262 us
  blocking collectives  71.3 us (27%)
  waiting for transfers between devices  68.2 us (26%)
  local copies, waits for them, and re-layouts  32.8 us (12%)
  starting transfers between devices  26.9 us (10%)
  matrix products  21.1 us (8%)
  other arithmetic  17.1 us (7%)
  between operations  13.9 us (5%)
  loops' own time  10.7 us (4%)
    unnamed x4, waiting for transfers between devices  68.2 us
    all_to_all x1, blocking collectives, body(): lax.all_to_all(send_buffer.reshape(n_seq, capacity, quarter), 'seq', spli...  51.5 us
    ppermute x8, starting transfers between devices, shifted(): return lax.ppermute(block, axis, route)  26.9 us
    unnamed x29, local copies, waits for them, and re-layouts  15.9 us
    all_to_all x1, blocking collectives, body(): lax.all_to_all(jnp.stack([normed_share] * lax.axis_size('grp')), 'grp', 0...  13.2 us
    another operation x1, loops' own time, body(): lax.map(attend, jnp.arange(patch_dev * heads_dev * block_count, dtype=jnp...  10.7 us
    dot_general x4, matrix products, attend(): jnp.dot(exponent.astype(jnp.bfloat16), value_block, preferred_element_typ...  8.91 us
    dot_general x4, matrix products, attend(): lax.dot_general(query_block, key_block, (((1,), (1,)), ((), ())), preferr...  7.2 us
  transfers between devices with their start and end apart: 10, of which 2 were waited for; matrix products, arithmetic and copies ran while one was open for 5% of the time, Pallas kernels for 0%

profile of v1, /device:TPU:33, one launch (start us, length us, event | category | flops | bytes accessed | tf_op | source)
XLA Modules:
  0.0 262.1 jit_solution(10282448863749288252)
XLA Ops:
  9.4 2.0 fusion.36
  13.7 3.2 %collective-permute-start = (bf16[1024,128]{0,1:T(8,128)(2,1)S(1)}, bf16[1024,128]{0,1:T(8,128)(2,1)}, u32[]{:S(2)}, u32[]{:S(2)}) collective-permute-start(bf16[1024,128]{0,1:T(8,128)(2,1)S(1)} %fusion.50), channel_id=1, source_target_pairs={{0,8},{4,12},{8,16},{12,20},{16,24},{20,28},{24,32},{28,36},{32,40... | collective-permute-start | bytes 786440 | tf_op jit(solution)/shard_map/ppermute | solution.py:14
  16.9 4.0 %collective-permute-start.1 = (bf16[1024,128]{0,1:T(8,128)(2,1)S(1)}, bf16[1024,128]{0,1:T(8,128)(2,1)}, u32[]{:S(2)}, u32[]{:S(2)}) collective-permute-start(bf16[1024,128]{0,1:T(8,128)(2,1)S(1)} %fusion.50), channel_id=1, source_target_pairs={{0,4},{4,8},{8,12},{12,16},{16,20},{20,24},{24,28},{28,32},{32,36}... | collective-permute-start | bytes 786440 | tf_op jit(solution)/shard_map/ppermute | solution.py:14
  21.0 1.9 collective-permute-start.2
  22.9 4.2 %collective-permute-start.3 = (bf16[1024,128]{0,1:T(8,128)(2,1)S(1)}, bf16[1024,128]{0,1:T(8,128)(2,1)}, u32[]{:S(2)}, u32[]{:S(2)}) collective-permute-start(bf16[1024,128]{0,1:T(8,128)(2,1)S(1)} %fusion.50), channel_id=1, source_target_pairs={{8,0},{12,4},{16,8},{20,12},{24,16},{28,20},{32,24},{36,28},{40,32... | collective-permute-start | bytes 786440 | tf_op jit(solution)/shard_map/ppermute | solution.py:14
  27.9 1.9 collective-permute-start.4
  31.2 3.9 %collective-permute-start.5 = (bf16[1024,128]{0,1:T(8,128)(2,1)}, bf16[1024,128]{0,1:T(8,128)(2,1)S(1)}, u32[]{:S(2)}, u32[]{:S(2)}) collective-permute-start(bf16[1024,128]{0,1:T(8,128)(2,1)} %fusion.53), channel_id=1, source_target_pairs={{0,4},{4,8},{8,12},{12,16},{16,20},{20,24},{24,28},{28,32},{32,36}... | collective-permute-start | bytes 786440 | tf_op jit(solution)/shard_map/ppermute | solution.py:14
  36.1 2.3 collective-permute-start.6
  39.4 5.4 %collective-permute-start.7 = (bf16[1024,128]{0,1:T(8,128)(2,1)}, bf16[1024,128]{0,1:T(8,128)(2,1)S(1)}, u32[]{:S(2)}, u32[]{:S(2)}) collective-permute-start(bf16[1024,128]{0,1:T(8,128)(2,1)} %fusion.53), channel_id=1, source_target_pairs={{8,0},{12,4},{16,8},{20,12},{24,16},{28,20},{32,24},{36,28},{40,32... | collective-permute-start | bytes 786440 | tf_op jit(solution)/shard_map/ppermute | solution.py:14
  55.4 2.4 copy.27
  58.5 2.0 gather_fusion.1
  60.5 39.8 %while.13 = (s32[]{:T(128)}, bf16[4,512,64]{1,2,0:T(8,128)(2,1)S(1)}, s32[4]{0:T(128)S(1)}, bf16[1,2,512,128]{2,1,3,0:T(2,128)(2,1)S(1)}, bf16[1,3072,128]{2,1,0...) while((s32[]{:T(128)}, ...), condition=%wide.region_10.11_spmd, body=%wide.region_7.10_spmd.sunk | while | flops 415300672 | bytes 20851312 | solution.py:93
  64.7 1.8 multiply_reduce_fusion.2
  68.3 2.2 fusion.79
  78.2 2.2 fusion.79
  88.2 2.2 fusion.79
  98.2 2.2 fusion.79
  102.6 34.9 %reduce-scatter.7.cloned.1.call-done = bf16[128,1024]{1,0:T(8,128)(2,1)} async-done(((bf16[512,1024]{1,0:T(8,128)(2,1)}), bf16[128,1024]{1,0:T(8,128)(2,1)}) %reduce-scatter.7.cloned.1.call-update) | async-done | bytes 262160
  140.0 6.6 %all-reduce = (f32[1024]{0:T(1024)S(1)}, f32[1024]{0:T(1024)S(1)}) all-reduce(f32[1024]{0:T(1024)S(1)} %get-tuple-element.144, f32[1024]{0:T(1024)S(1)} %get-tuple-element.143), channel_id=1, replica_groups=mesh['seq'=128,'grp'=4] {'grp'}, use_global_device_ids=true, to_apply=%region_15.16 | all-reduce | flops 2048 | bytes 16384 | tf_op jit(solution)/shard_map/psum | solution.py:106
  147.2 13.2 %all_to_all.10 = bf16[4,1024,128]{1,2,0:T(8,128)(2,1)S(1)} all-to-all(bf16[4,1024,128]{1,2,0:T(8,128)(2,1)S(1)} %stack.2), channel_id=1, replica_groups=mesh['seq'=128,'grp'=4] {'grp'}, dimensions={0} | all-to-all | bytes 2097152 | tf_op jit(solution)/shard_map/all_to_all | solution.py:116
  160.4 2.5 convolution_convert_fusion.1
  165.3 33.2 %reduce-scatter.9.cloned.1.call-done = bf16[128,1024]{1,0:T(8,128)(2,1)} async-done(((bf16[512,1024]{1,0:T(8,128)(2,1)}), bf16[128,1024]{1,0:T(8,128)(2,1)}) %reduce-scatter.9.cloned.1.call-update) | async-done | bytes 262160
  199.6 3.4 %scatter_custom_fusion = bf16[2048,128]{1,0:T(8,128)(2,1)S(1)} fusion(s32[1024]{0:T(1024)S(1)} %bitcast.118, bf16[1024,128]{1,0:T(8,128)(2,1)S(1)} %get-tuple-element.161, bf16[1024,128]{1,0:T(8,128)(2,1)S(1)} %copy.34, bf16[]{:T(256)} %constant.173.clone.1), kind=kCustom, calls=%fused_computation.67 | custom fusion | flops 524288 | bytes 1048578 | tf_op jit(solution)/shard_map/scatter | solution.py:133
  203.0 51.5 %all_to_all.11 = bf16[128,16,128]{2,1,0:T(8,128)(2,1)S(1)} all-to-all(bf16[128,16,128]{2,1,0:T(8,128)(2,1)S(1)} %bitcast.106), channel_id=1, replica_groups=mesh['seq'=128,'grp'=4] {'seq'}, dimensions={0} | all-to-all | bytes 1048576 | tf_op jit(solution)/shard_map/all_to_all | solution.py:134
  (102 shorter events, 48.1 us)
Async XLA Ops:
  6.5 94.2 %copy-start = (bf16[512,512]{1,0:T(8,128)(2,1)S(1)}, bf16[512,512]{1,0:T(8,128)(2,1)}, u32[]{:S(2)}) copy-start(bf16[512,512]{1,0:T(8,128)(2,1)} %param.12) | copy-start | bytes 1572868
  6.5 131.0 %reduce-scatter.7.cloned.1.call-start = ((), (), s32[]{:S(2)}) async-start(), calls=%async_computation.4 | async-start | bytes 1310720
  11.4 16.5 %copy-start.1 = (f32[1024,384]{0,1}, f32[1024,384]{0,1:S(1)}, u32[]{:S(2)}) copy-start(f32[1024,384]{0,1:S(1)} %fusion.36) | copy-start | bytes 4718596
  13.7 17.2 %copy-start.5 = (f32[2]{0:T(128)S(1)}, f32[2]{0:T(128)}, u32[]{:S(2)}) copy-start(f32[2]{0:T(128)} %param.15) | copy-start | bytes 28
  13.7 17.5 %collective-permute-start = (bf16[1024,128]{0,1:T(8,128)(2,1)S(1)}, bf16[1024,128]{0,1:T(8,128)(2,1)}, u32[]{:S(2)}, u32[]{:S(2)}) collective-permute-start(bf16[1024,128]{0,1:T(8,128)(2,1)S(1)} %fusion.50), channel_id=1, source_target_pairs={{0,8},{4,12},{8,16},{12,20},{16,24},{20,28},{24,32},{28,36},{32,40... | collective-permute-start | bytes 786440 | tf_op jit(solution)/shard_map/ppermute | solution.py:14
  16.9 19.2 %collective-permute-start.1 = (bf16[1024,128]{0,1:T(8,128)(2,1)S(1)}, bf16[1024,128]{0,1:T(8,128)(2,1)}, u32[]{:S(2)}, u32[]{:S(2)}) collective-permute-start(bf16[1024,128]{0,1:T(8,128)(2,1)S(1)} %fusion.50), channel_id=1, source_target_pairs={{0,4},{4,8},{8,12},{12,16},{16,20},{20,24},{24,28},{28,32},{32,36}... | collective-permute-start | bytes 786440 | tf_op jit(solution)/shard_map/ppermute | solution.py:14
  21.0 25.5 %collective-permute-start.2 = (bf16[1024,128]{0,1:T(8,128)(2,1)S(1)}, bf16[1024,128]{0,1:T(8,128)(2,1)}, u32[]{:S(2)}, u32[]{:S(2)}) collective-permute-start(bf16[1024,128]{0,1:T(8,128)(2,1)S(1)} %fusion.50), channel_id=1, source_target_pairs={{4,0},{8,4},{12,8},{16,12},{20,16},{24,20},{28,24},{32,28},{36,32}... | collective-permute-start | bytes 786440 | tf_op jit(solution)/shard_map/ppermute | solution.py:14
  22.9 24.5 %collective-permute-start.3 = (bf16[1024,128]{0,1:T(8,128)(2,1)S(1)}, bf16[1024,128]{0,1:T(8,128)(2,1)}, u32[]{:S(2)}, u32[]{:S(2)}) collective-permute-start(bf16[1024,128]{0,1:T(8,128)(2,1)S(1)} %fusion.50), channel_id=1, source_target_pairs={{8,0},{12,4},{16,8},{20,12},{24,16},{28,20},{32,24},{36,28},{40,32... | collective-permute-start | bytes 786440 | tf_op jit(solution)/shard_map/ppermute | solution.py:14
  27.9 11.5 %collective-permute-start.4 = (bf16[1024,128]{0,1:T(8,128)(2,1)}, bf16[1024,128]{0,1:T(8,128)(2,1)}, u32[]{:S(2)}, u32[]{:S(2)}) collective-permute-start(bf16[1024,128]{0,1:T(8,128)(2,1)} %fusion.53), channel_id=1, source_target_pairs={{0,8},{4,12},{8,16},{12,20},{16,24},{20,28},{24,32},{28,36},{32,40... | collective-permute-start | bytes 786440 | tf_op jit(solution)/shard_map/ppermute | solution.py:14
  29.8 1.3 copy-start.6
  31.2 17.3 %collective-permute-start.5 = (bf16[1024,128]{0,1:T(8,128)(2,1)}, bf16[1024,128]{0,1:T(8,128)(2,1)S(1)}, u32[]{:S(2)}, u32[]{:S(2)}) collective-permute-start(bf16[1024,128]{0,1:T(8,128)(2,1)} %fusion.53), channel_id=1, source_target_pairs={{0,4},{4,8},{8,12},{12,16},{16,20},{20,24},{24,28},{28,32},{32,36}... | collective-permute-start | bytes 786440 | tf_op jit(solution)/shard_map/ppermute | solution.py:14
  36.1 17.7 %collective-permute-start.6 = (bf16[1024,128]{0,1:T(8,128)(2,1)}, bf16[1024,128]{0,1:T(8,128)(2,1)S(1)}, u32[]{:S(2)}, u32[]{:S(2)}) collective-permute-start(bf16[1024,128]{0,1:T(8,128)(2,1)} %fusion.53), channel_id=1, source_target_pairs={{4,0},{8,4},{12,8},{16,12},{20,16},{24,20},{28,24},{32,28},{36,32}... | collective-permute-start | bytes 786440 | tf_op jit(solution)/shard_map/ppermute | solution.py:14
  39.4 15.2 %collective-permute-start.7 = (bf16[1024,128]{0,1:T(8,128)(2,1)}, bf16[1024,128]{0,1:T(8,128)(2,1)S(1)}, u32[]{:S(2)}, u32[]{:S(2)}) collective-permute-start(bf16[1024,128]{0,1:T(8,128)(2,1)} %fusion.53), channel_id=1, source_target_pairs={{8,0},{12,4},{16,8},{20,12},{24,16},{28,20},{32,24},{36,28},{40,32... | collective-permute-start | bytes 786440 | tf_op jit(solution)/shard_map/ppermute | solution.py:14
  48.4 1.1 copy-start.2
  102.5 96.0 %reduce-scatter.9.cloned.1.call-start = ((), (), s32[]{:S(2)}) async-start(), calls=%async_computation.5 | async-start | bytes 1310720
  146.9 13.5 %copy-start.4 = (bf16[512,512]{1,0:T(8,128)(2,1)S(1)}, bf16[512,512]{1,0:T(8,128)(2,1)}, u32[]{:S(2)}) copy-start(bf16[512,512]{1,0:T(8,128)(2,1)} %param.14) | copy-start | bytes 1572868
  163.0 1.4 copy-start.3
Sparse Core Ops, SparseCore 0:
  102.7 34.8 reduce-scatter.6
  164.5 33.9 reduce-scatter.8
